TPU v7x, 512 devices: a whole 4x4x16 slice. The times are simulated.
512 devices in a mesh: inst: 8 (over y, core), space: 64 (over x, z).
Axes of the slice: x: 4, y: 4, z: 16, core: 2. Of those that a mesh axis runs over, the one named last changes fastest.
Arguments:
- amplitudes: float32 [8, 40], replicated, may hold values from -6 to 6
- modal_coeffs: float32 [40, 3, 4096], P(None, None, ('inst', 'space')), may hold values from -0.6 to 0.6
- centre_positions: float32 [3, 4096], P(None, ('inst', 'space')), may hold values from 0 to 256
- base_nodes: float32 [3, 128, 64, 256], P(None, 'space'), may hold values from -1 to 256
Outputs:
- displacement: float32 [8, 3, 128, 64, 256], P('inst', None, 'space')
- metrics: float32 [8, 10, 128, 64, 256], P('inst', None, 'space')
All inputs are finite; a program needn't handle non-finite values.
Results may differ from a plain program's by a relative error of at most 0.0003.
Values sent between devices are 32-bit elements; how exact they have to be, the bound alone decides.
A program may use at most 64 MiB of HBM per device.

v0:
```python
import jax
import jax.numpy as jnp
from jax import lax
from jax.experimental import pallas as pl
from jax.experimental.pallas import tpu as pltpu
from jax.sharding import PartitionSpec as P

MESH = pl.DeviceIdType.MESH
HIGH = lax.Precision.HIGHEST
XS, YS, ZS, CORES = 4, 4, 16, 2
INST, SPACE = YS * CORES, XS * ZS
OWN = 8
BLOCKS = XS * YS * CORES
NC = BLOCKS * ZS * OWN
VALUES = 32
BINS = 32
CHUNK = 128
GROUP = 8
PLACED = 256
GROUPS = (NC + PLACED) // 32
MARGIN = 1.0 + 2.0**-11
VMEM_LIMIT = 32 * 1024 * 1024


def vmem():
    return pl.BlockSpec(memory_space=pltpu.VMEM)


def params(**more):
    return pltpu.CompilerParams(vmem_limit_bytes=VMEM_LIMIT, **more)


def swap_blocks(arrays):
    block = lax.broadcasted_iota(jnp.int32, arrays[0].shape, 1) // 16
    arrays = list(arrays)
    for step in (1, 2, 4):
        upper = (block & step) != 0
        for a in range(8):
            if not a & step:
                one, two = arrays[a], arrays[a | step]
                arrays[a] = jnp.where(upper, pltpu.roll(two, 16 * step, 1), one)
                arrays[a | step] = jnp.where(upper, two, pltpu.roll(one, 128 - 16 * step, 1))
    return arrays


def gather_kernel(own_ref, out_ref, zbuf, send, recv):
    inst, space = lax.axis_index("inst"), lax.axis_index("space")
    y, core = inst // CORES, inst % CORES
    x, z = space // ZS, space % ZS
    z_peers = [(inst, x * ZS + lax.rem(z + k, ZS)) for k in range(1, ZS)]
    steps = [(a, b) for a in range(YS) for b in range(XS) if a or b]
    plane_peers = [
        (lax.rem(y + a, YS) * CORES + core, lax.rem(x + b, XS) * ZS + z) for a, b in steps
    ]
    other = (y * CORES + (1 - core), space)

    def hops(a, b, c):
        return min(a, ZS - a) + min(b, YS - b) + min(c, XS - c)

    z_order = sorted(range(ZS - 1), key=lambda k: -hops(k + 1, 0, 0))
    plane_order = sorted(range(len(steps)), key=lambda k: -hops(0, *steps[k]))
    peers = [z_peers[k] for k in z_order] + [plane_peers[k] for k in plane_order] + [other]
    barrier = pltpu.get_barrier_semaphore()
    for peer in peers:
        pl.semaphore_signal(barrier, inc=1, device_id=peer, device_id_type=MESH)

    transposed = (((1,), (1,)), ((), ()))

    def high_dot(a, b):
        return lax.dot_general(a, b, transposed, precision=HIGH, preferred_element_type=jnp.float32)

    amp = own_ref[24:32]
    eye = (
        lax.broadcasted_iota(jnp.int32, (OWN, OWN), 0) == lax.broadcasted_iota(jnp.int32, (OWN, OWN), 1)
    ).astype(jnp.float32)
    own = [high_dot(own_ref[8 * c : 8 * c + 8], amp) for c in range(3)]
    own.append(high_dot(eye, own_ref[32:40, 0:OWN])[:, 0:3])
    own = jnp.concatenate(own + [jnp.zeros((OWN, 128 - 27), jnp.float32)], axis=1)
    row_id = lax.broadcasted_iota(jnp.int32, (OWN, 128), 0) % 4
    spread = jnp.zeros((OWN, 128), jnp.float32)
    for a in range(4):
        moved = own if a == 0 else pltpu.roll(own, VALUES * a, 1)
        spread = spread + jnp.where(row_id == a, moved, 0.0)
    zbuf[z] = jnp.concatenate(
        [
            jnp.sum(spread[0:4], axis=0, keepdims=True),
            jnp.sum(spread[4:8], axis=0, keepdims=True),
        ],
        axis=0,
    )

    pl.semaphore_wait(barrier, len(peers))

    def start(ref, k, peer):
        copy = pltpu.make_async_remote_copy(
            src_ref=ref,
            dst_ref=ref,
            send_sem=send.at[k],
            recv_sem=recv.at[k],
            device_id=peer,
            device_id_type=MESH,
        )
        copy.start()
        return copy

    copies = [start(zbuf.at[z], k, z_peers[k]) for k in z_order]
    for copy in reversed(copies):
        copy.wait()
    rows = jnp.concatenate([zbuf[i] for i in range(ZS)], axis=0)
    rows = jnp.concatenate([rows, jnp.zeros((128 - 2 * ZS, 128), jnp.float32)], axis=0).T
    block = rows[0:VALUES]
    for a in range(1, 4):
        block = block + pltpu.roll(rows[VALUES * a : VALUES * (a + 1)], VALUES * a, 1)
    mine = core * (XS * YS) + y * XS + x
    out_ref[mine] = block

    copies = [start(out_ref.at[mine], ZS - 1 + k, plane_peers[k]) for k in plane_order]
    passed = [start(out_ref.at[mine], ZS - 1 + len(steps), other)]
    for copy, k in reversed(list(zip(copies, plane_order))):
        copy.wait_recv()
        a, b = steps[k]
        origin = core * (XS * YS) + lax.rem(y + YS - a, YS) * XS + lax.rem(x + XS - b, XS)
        passed.append(start(out_ref.at[origin], ZS + len(steps) + k, other))
    for copy in copies:
        copy.wait_send()
    for copy in passed:
        copy.wait()


def gather(own):
    count = ZS + 2 * XS * YS - 2
    return pl.pallas_call(
        gather_kernel,
        out_shape=jax.ShapeDtypeStruct((BLOCKS, VALUES, 128), jnp.float32),
        in_specs=[vmem()],
        out_specs=vmem(),
        scratch_shapes=[
            pltpu.VMEM((ZS, 2, 128), jnp.float32),
            pltpu.SemaphoreType.DMA((count,)),
            pltpu.SemaphoreType.DMA((count,)),
        ],
        compiler_params=params(collective_id=0, has_side_effects=True),
        cost_estimate=pl.CostEstimate(flops=10**9, bytes_accessed=2 * 10**7, transcendentals=0),
        name="gather",
    )(own)


def whole_dot(a, b, precision=None):
    return jnp.dot(a, b, precision=precision, preferred_element_type=jnp.float32)


def window(tiles, centres, windows, t, place):
    spot = [
        jnp.concatenate([centres[c * GROUPS + place + k] for k in range(4)], axis=0) for c in range(3)
    ]
    pieces = windows[place]
    tops, rests = [], []
    for p in range(2):
        square = None
        for c in range(3):
            gap = spot[c] - tiles[t, 2 * c + p : 2 * c + p + 1, :]
            square = gap * gap if square is None else square + gap * gap
        radius = square * lax.rsqrt(jnp.maximum(square, 1e-30))
        rest = jnp.maximum(1.0 - radius, 0.0)
        rest = rest * rest
        value = rest * rest * (4.0 * radius + 1.0)
        top = value.astype(jnp.bfloat16)
        tops.append(top)
        rests.append((value - top.astype(jnp.float32)).astype(jnp.bfloat16))
    full = whole_dot(pieces, jnp.concatenate(tops, axis=1))
    extra = whole_dot(pieces[0:32], jnp.concatenate(rests, axis=1))
    return full[0:24] + (full[24:48] + extra[0:24])


def evaluate_kernel(g_ref, n_ref, windows, centres, tiles, found, edges, kept, nodes, parts, order, weights, ends, arrived, passing):
    keep = pltpu.make_async_copy(n_ref, kept, passing)
    keep.start()
    first = pl.multiple_of(lax.axis_index("inst") * 8, 8)
    nodes[...] = n_ref[:, :, pl.ds(first, 8), :] * 0.25

    for half in range(2):
        lanes = slice(half * 128, half * 128 + 128)
        rows = [
            jnp.concatenate(
                [nodes[c, p, j : j + 1, lanes] for c in range(3) for p in range(2)]
                + [jnp.zeros((2, 128), jnp.float32)],
                axis=0,
            )
            for j in range(8)
        ]
        for t, tile in enumerate(swap_blocks(rows)):
            tiles[8 * half + t] = tile
    spots = [g_ref[:, 24 + c, :] * 0.25 for c in range(3)]
    near = None
    for c in range(3):
        low = jnp.min(nodes[c]) - MARGIN
        high = jnp.max(nodes[c]) + MARGIN
        inside = (spots[c] >= low) & (spots[c] <= high)
        near = inside if near is None else near & inside
        if c == 2:
            k_low, scale = low, BINS / jnp.full((1, 1), high - low)

    def bin_of(value):
        return jnp.clip(jnp.floor((value - k_low) * scale), 0.0, BINS - 1.0)

    bins = jnp.where(near, bin_of(spots[2]), -1.0)

    bin_id = lax.broadcasted_iota(jnp.int32, (BINS, 128), 0).astype(jnp.float32)
    member = jnp.concatenate(
        [(bins[i : i + 1] == bin_id).astype(jnp.float32) for i in range(BLOCKS)], axis=0
    )
    lane = lax.broadcasted_iota(jnp.int32, (128, 256), 1)
    counting = ((lax.broadcasted_iota(jnp.int32, (128, 256), 0) <= lane) | (lane >= 128)).astype(jnp.float32)
    counts = whole_dot(member.astype(jnp.bfloat16), counting.astype(jnp.bfloat16))
    total = counts[0:BINS, 128:256]
    for i in range(1, BLOCKS):
        total = total + counts[i * BINS : (i + 1) * BINS, 128:256]
    earlier = (
        lax.broadcasted_iota(jnp.int32, (BINS, BINS), 1) < lax.broadcasted_iota(jnp.int32, (BINS, BINS), 0)
    ).astype(jnp.float32)
    running = whole_dot(earlier, total, HIGH)
    rows = []
    for i in range(BLOCKS):
        own = slice(i * BINS, (i + 1) * BINS)
        rows.append(jnp.sum(member[own] * (running + counts[own, 0:128]), axis=0, keepdims=True) - 1.0)
        running = running + counts[own, 128:256]
    position = jnp.concatenate(rows + [jnp.zeros((128 - BLOCKS, 128), jnp.float32)], axis=0).T
    for i in range(BLOCKS):
        order[i * 128 : i * 128 + 128, :] = jnp.broadcast_to(position[:, i : i + 1], (128, 128))

    k_min = jnp.min(jnp.min(nodes[2], axis=0), axis=0, keepdims=True)
    k_max = jnp.max(jnp.max(nodes[2], axis=0), axis=0, keepdims=True)
    for step in (1, 2, 4, 8):
        k_min = jnp.minimum(k_min, pltpu.roll(k_min, step, 1))
        k_max = jnp.maximum(k_max, pltpu.roll(k_max, step, 1))
    wide_id = lax.broadcasted_iota(jnp.int32, (BINS, 256), 0).astype(jnp.float32)
    wide_total = jnp.concatenate([total, total], axis=1)
    start = jnp.sum(jnp.where(wide_id < bin_of(k_min - MARGIN), wide_total, 0.0), axis=0, keepdims=True)
    stop = jnp.sum(jnp.where(wide_id <= bin_of(k_max + MARGIN), wide_total, 0.0), axis=0, keepdims=True)
    begin = jnp.floor(start * (1.0 / 32.0))
    count = jnp.floor((jnp.maximum(stop - 32.0 * begin, 1.0) + (CHUNK - 1.0)) * (1.0 / CHUNK))
    edges[0:1, :] = begin.astype(jnp.int32)
    edges[1:2, :] = count.astype(jnp.int32)
    at_tile = lax.broadcasted_iota(jnp.int32, (1, 256), 1) % 16 == 15
    more = at_tile & (count > 1.0)
    tile_id = lax.broadcasted_iota(jnp.int32, (1, 256), 1) // 16
    lowest = jnp.min(jnp.where(more, tile_id, 16), axis=1, keepdims=True)
    highest = jnp.max(jnp.where(more, tile_id + 1, 0), axis=1, keepdims=True)
    edges[2:3, :] = jnp.broadcast_to(lowest, (1, 256))
    edges[3:4, :] = jnp.broadcast_to(highest, (1, 256))
    copy = pltpu.make_async_copy(edges, ends, arrived)
    copy.start()
    chunks = (jnp.sum(total[:, 0:1]).astype(jnp.int32) + (PLACED - 1)) // PLACED

    def split(i, carry):
        for half in range(2):
            value = g_ref[2 * i + half]
            motion = value[0:24]
            top = motion.astype(jnp.bfloat16).astype(jnp.float32)
            spot = value[24:32] * 0.25
            one = spot.astype(jnp.bfloat16).astype(jnp.float32)
            two = (spot - one).astype(jnp.bfloat16).astype(jnp.float32)
            three = spot - one - two
            parts[i, :, half * 128 : half * 128 + 128] = jnp.concatenate(
                [top, motion - top, one, two, three, jnp.zeros((8, 128), jnp.float32)], axis=0
            ).astype(jnp.bfloat16)
        return carry

    lax.fori_loop(0, BLOCKS // 2, split, 0)

    slot = lax.broadcasted_iota(jnp.int32, (1, 128), 1)

    def place_chunk(s, carry):
        sums = jnp.zeros((80, PLACED), jnp.float32)
        wanted = [(slot + (s * PLACED + 128 * half)).astype(jnp.float32) for half in range(2)]
        for i in range(BLOCKS // 2):
            at = order[i * 256 : i * 256 + 256, :]
            hit = jnp.concatenate([jnp.where(at == w, 1.0, 0.0) for w in wanted], axis=1)
            sums = sums + whole_dot(parts[i], hit.astype(jnp.bfloat16))
        short = sums[0:48]
        spot = (sums[48:56] + sums[56:64]) + sums[64:72]
        for half in range(2):
            lanes = slice(half * 128, half * 128 + 128)
            weights[2 * s + half] = short[:, lanes]
            piece = jnp.concatenate([spot[:, lanes], jnp.zeros((120, 128), jnp.float32)], axis=0).T
            for c in range(3):
                into = pl.ds(c * GROUPS + s * 8 + half * 4, 4)
                centres[into] = jnp.broadcast_to(piece[:, c : c + 1], (128, 128)).reshape(4, 32, 128)
        return carry

    lax.fori_loop(0, chunks, place_chunk, 0)

    behind = 2 * chunks
    for half in range(2):
        weights[behind + half] = jnp.zeros((48, CHUNK), jnp.float32)
        for c in range(3):
            centres[pl.ds(c * GROUPS + 4 * (behind + half), 4)] = jnp.zeros((4, 32, 128), jnp.float32)
    lane = lax.broadcasted_iota(jnp.int32, (48, CHUNK), 1)

    def shift_chunks(s, carry):
        values = [weights[2 * s + k] for k in range(3)]
        for k in range(2):
            place = 4 * (2 * s + k)
            windows[place] = values[k].astype(jnp.bfloat16)
            for r in range(1, 4):
                back = CHUNK - 32 * r
                moved = jnp.where(lane < back, pltpu.roll(values[k], back, 1), pltpu.roll(values[k + 1], back, 1))
                windows[place + r] = moved.astype(jnp.bfloat16)
        return carry

    lax.fori_loop(0, chunks, shift_chunks, 0)
    for r in range(4):
        windows[4 * behind + r] = jnp.zeros((48, CHUNK), jnp.bfloat16)

    found[...] = jnp.zeros_like(found)
    copy.wait()

    def more_windows(t, carry):
        def one(k, carry):
            found[t] += window(tiles, centres, windows, t, ends[0, 16 * t + 15] + 4 * k)
            return carry

        return lax.fori_loop(1, ends[1, 16 * t + 15], one, carry)

    lax.fori_loop(ends[2, 0], ends[3, 0], more_windows, 0)
    keep.wait()


def evaluate(gathered, base_nodes):
    shape = jax.ShapeDtypeStruct
    return pl.pallas_call(
        evaluate_kernel,
        out_shape=(
            shape((4 * (NC // CHUNK + 1), 48, CHUNK), jnp.bfloat16),
            shape((3 * GROUPS, 32, 128), jnp.float32),
            shape((16, 8, 128), jnp.float32),
            shape((16, 24, 256), jnp.float32),
            shape((8, 256), jnp.int32),
            shape(base_nodes.shape, jnp.float32),
        ),
        in_specs=[vmem()] * 2,
        out_specs=(vmem(),) * 6,
        scratch_shapes=[
            pltpu.VMEM((3, 2, 8, 256), jnp.float32),
            pltpu.VMEM((BLOCKS // 2, 80, 256), jnp.bfloat16),
            pltpu.VMEM((NC, 128), jnp.float32),
            pltpu.VMEM((NC // CHUNK + 2, 48, CHUNK), jnp.float32),
            pltpu.SMEM((8, 256), jnp.int32),
            pltpu.SemaphoreType.DMA,
            pltpu.SemaphoreType.DMA,
        ],
        compiler_params=params(),
        name="evaluate",
    )(gathered, base_nodes)


def exchange_kernel(windows, centres, tiles, more, edges, n_ref, own, halo, found, moved, deformed, send, recv, send_on, recv_on):
    inst, space = lax.axis_index("inst"), lax.axis_index("space")
    behind, ahead = lax.rem(space + SPACE - 1, SPACE), lax.rem(space + 1, SPACE)
    y, core = inst // CORES, inst % CORES

    def device(a, other):
        return lax.rem(y + a, YS) * CORES + (1 - core if other else core)

    order = [(0, 1)] + [(a, other) for a in (1, YS - 1, 2) for other in (0, 1)]
    peers = [(device(*step), space) for step in order] + [(inst, behind), (inst, ahead)]
    barrier = pltpu.get_barrier_semaphore()
    for peer in peers:
        pl.semaphore_signal(barrier, inc=1, device_id=peer, device_id_type=MESH)

    def start(source, target, sent, arrived, device):
        copy = pltpu.make_async_remote_copy(
            src_ref=source,
            dst_ref=target,
            send_sem=sent,
            recv_sem=arrived,
            device_id=device,
            device_id_type=MESH,
        )
        copy.start()
        return copy

    def first_windows(group, carry):
        for k in range(GROUP):
            t = group * GROUP + k
            found[t] = more[t] + window(tiles, centres, windows, t, edges[0, 16 * t + 15])
        return carry

    lax.fori_loop(0, 16 // GROUP, first_windows, 0)
    for p in range(2):
        for half in range(2):
            rows = swap_blocks([found[8 * half + t, :, p * 128 : p * 128 + 128] for t in range(8)])
            for j in range(8):
                for c in range(3):
                    into = pl.ds(c * 32 + p * 16 + half * 8 + j, 8, stride=96)
                    moved[into, :] = rows[j][c * 8 : c * 8 + 8]

    def add_nodes(strip):
        rows = pl.ds(pl.multiple_of(strip * 8, 8), 8)
        for c in range(3):
            for p in range(2):
                nodes = n_ref[c, p, rows, :]
                for half in range(2):
                    at, to = c * 32 + p * 16 + half * 8, c * 16 + half * 8
                    lanes = slice(half * 128, half * 128 + 128)
                    deformed[p, strip, to : to + 8, :] = own[strip, at : at + 8, :] + nodes[:, lanes]

    def pass_on(k, chip):
        strips = pl.ds(CORES * chip, CORES)
        return [
            start(
                deformed.at[side, strips],
                halo.at[1 - side, strips],
                send_on.at[side, k],
                recv_on.at[side, k],
                (inst, (behind, ahead)[side]),
            )
            for side in range(2)
        ]

    def rows_for(target):
        return pl.ds(pl.multiple_of(target * 96, 96), 96)

    own[inst] = moved[rows_for(inst), :]
    add_nodes(inst)
    pl.semaphore_wait(barrier, len(peers))
    copies = [
        start(moved.at[rows_for(peer[0])], own.at[inst], send.at[k], recv.at[k], peer)
        for k, peer in enumerate(peers[: len(order)])
    ]
    passed = []
    for k, a in enumerate((0, 1, YS - 1, 2)):
        for copy, step in zip(copies, order):
            if step[0] == a:
                copy.wait_recv()
                add_nodes(device(YS - a, step[1]))
        passed += pass_on(k, lax.rem(y + YS - a, YS))
    for copy in copies:
        copy.wait_send()
    for copy in passed:
        copy.wait()


def exchange(*arrays):
    return pl.pallas_call(
        exchange_kernel,
        out_shape=(
            jax.ShapeDtypeStruct((INST, 96, 128), jnp.float32),
            jax.ShapeDtypeStruct((2, INST, 48, 128), jnp.float32),
        ),
        in_specs=[vmem()] * 4 + [pl.BlockSpec(memory_space=pltpu.SMEM), vmem()],
        out_specs=(vmem(), vmem()),
        scratch_shapes=[
            pltpu.VMEM((16, 24, 256), jnp.float32),
            pltpu.VMEM((INST * 96, 128), jnp.float32),
            pltpu.VMEM((2, INST, 48, 128), jnp.float32),
            pltpu.SemaphoreType.DMA((INST,)),
            pltpu.SemaphoreType.DMA((INST,)),
            pltpu.SemaphoreType.DMA((2, YS)),
            pltpu.SemaphoreType.DMA((2, YS)),
        ],
        compiler_params=params(collective_id=1, has_side_effects=True),
        name="exchange",
    )(*arrays)


def shifted(value, axis):
    extent = value.shape[axis]
    at = lax.broadcasted_iota(jnp.int32, value.shape, axis)
    following = pltpu.roll(value, extent - 1, axis)
    preceding = pltpu.roll(value, 1, axis)
    upper = jnp.where(at == extent - 1, 2.0 * value - preceding, following)
    lower = jnp.where(at == 0, 2.0 * value - following, preceding)
    return (upper - lower) * 0.5


def cross(a, b):
    return [
        a[1] * b[2] - a[2] * b[1],
        a[2] * b[0] - a[0] * b[2],
        a[0] * b[1] - a[1] * b[0],
    ]


def metrics_kernel(own, halo, n_ref, disp_hbm, metrics_hbm, disp, ends, metrics, sems):
    space = lax.axis_index("space")
    copies = []

    def leave(source, target):
        copy = pltpu.make_async_copy(source, target, sems.at[len(copies)])
        copy.start()
        copies.append(copy)

    def strip_rows(strip, carry):
        rows = pl.ds(pl.multiple_of(strip * 8, 8), 8)
        for c in range(3):
            for half in range(2):
                lanes = slice(half * 128, half * 128 + 128)
                for p in range(2):
                    at = c * 32 + p * 16 + half * 8
                    disp[c, p, rows, lanes] = own[strip, at : at + 8, :]
                    at = c * 16 + half * 8
                    ends[p, c, rows, lanes] = halo[p, strip, at : at + 8, :]
        return carry

    lax.fori_loop(0, INST, strip_rows, 0, unroll=True)
    leave(disp, disp_hbm.at[0])

    for p in range(2):
        here = [n_ref[c, p] + disp[c, p] for c in range(3)]
        there = [n_ref[c, 1 - p] + disp[c, 1 - p] for c in range(3)]
        along_i = []
        for c in range(3):
            if p == 0:
                beyond = jnp.where(space == 0, 2.0 * here[c] - there[c], ends[0, c])
                along_i.append((there[c] - beyond) * 0.5)
            else:
                beyond = jnp.where(space == SPACE - 1, 2.0 * here[c] - there[c], ends[1, c])
                along_i.append((beyond - there[c]) * 0.5)
        along_j = [shifted(value, 0) for value in here]
        along_k = [shifted(value, 1) for value in here]
        one = cross(along_j, along_k)
        two = cross(along_k, along_i)
        three = cross(along_i, along_j)
        last = along_i[0] * one[0] + along_i[1] * one[1] + along_i[2] * one[2]
        row = 0
        for group in (one, two, three, [last]):
            for k, value in enumerate(group):
                metrics[p, row + k] = value
            rows = pl.ds(row, len(group))
            leave(metrics.at[p, rows], metrics_hbm.at[0, rows, p])
            row += len(group)
    for copy in copies:
        copy.wait()


def metric_rows(own, halo, base_nodes):
    anywhere = pl.BlockSpec(memory_space=pltpu.HBM)
    return pl.pallas_call(
        metrics_kernel,
        out_shape=(
            jax.ShapeDtypeStruct((1,) + base_nodes.shape, jnp.float32),
            jax.ShapeDtypeStruct((1, 10) + base_nodes.shape[1:], jnp.float32),
        ),
        in_specs=[vmem()] * 3,
        out_specs=(anywhere, anywhere),
        scratch_shapes=[
            pltpu.VMEM(base_nodes.shape, jnp.float32),
            pltpu.VMEM((2, 3) + base_nodes.shape[2:], jnp.float32),
            pltpu.VMEM((2, 10) + base_nodes.shape[2:], jnp.float32),
            pltpu.SemaphoreType.DMA((9,)),
        ],
        compiler_params=params(),
        name="metrics",
    )(own, halo, base_nodes)


def body(amplitudes, modal_coeffs, centre_positions, base_nodes):
    modes = amplitudes.shape[1]
    own = jnp.concatenate(
        [
            modal_coeffs.transpose(1, 2, 0).reshape(3 * OWN, modes),
            amplitudes,
            jnp.pad(centre_positions, ((0, 5), (0, modes - OWN))),
        ],
        axis=0,
    )
    gathered = gather(own)
    *placed, nodes = evaluate(gathered, base_nodes)
    own, halo = exchange(*placed, nodes)
    return metric_rows(own, halo, nodes)


def solution(mesh):
    in_specs = (
        P(),
        P(None, None, ("inst", "space")),
        P(None, ("inst", "space")),
        P(None, "space", None, None),
    )
    out_specs = (P("inst", None, "space", None, None), P("inst", None, "space", None, None))
    return jax.shard_map(body, mesh=mesh, in_specs=in_specs, out_specs=out_specs, check_vma=False)
```

profile of v0, /device:TPU:1, one launch (start us, length us, event | category | flops | bytes accessed | tf_op | source)
XLA Modules:
  0.0 54.5 jit_solution(7292271821588973179)
XLA Ops:
  0.6 0.7 %select_maximum_fusion.own_ref = f32[40,40]{1,0:T(8,128)S(1)} fusion(f32[3,8]{1,0:T(4,128)} %param.6, f32[8,40]{1,0:T(8,128)} %param.4, f32[24,40]{1,0:T(8,128)} %bitcast.3), kind=kLoop, calls=%fused_computation | loop fusion | flops 6400 | bytes 11616 | tf_op jit(solution)/shard_map/concatenate | solution.py:560
  1.4 0.0 copy-start
  1.4 31.0 %gather.1.g_ref = f32[32,32,128]{2,1,0:T(8,128)S(1)} custom-call(f32[40,40]{1,0:T(8,128)S(1)} %select_maximum_fusion.own_ref), custom_call_target="tpu_custom_call" | custom-call | flops 1000000000 | bytes 20000000 | tf_op jit(solution)/shard_map/gather/pallas_call | solution.py:132
  32.4 0.0 copy-done
  32.4 5.1 %evaluate.1 = (bf16[132,48,128]{2,1,0:T(8,128)(2,1)S(1)}, f32[408,32,128]{2,1,0:T(8,128)S(1)}, f32[16,8,128]{2,1,0:T(8,128)S(1)}, f32[16,24,256]{2,1,0:T(8,128)S...) custom-call(f32[32,32,128]{2,1,0:T(8,128)S(1)} %gather.1.g_ref, f32[3,2,64,256]{3,2,1,0:T(8,128)S(1)} %copy-done), custom_call_target="tpu_custom_call" | custom-call | tf_op jit(solution)/shard_map/evaluate/pallas_call | solution.py:331
  37.5 15.6 %exchange.1 = (f32[8,96,128]{2,1,0:T(8,128)S(1)}, f32[2,8,48,128]{3,2,1,0:T(8,128)S(1)}) custom-call(bf16[132,48,128]{2,1,0:T(8,128)(2,1)S(1)} %get-tuple-element.10.windows, f32[408,32,128]{2,1,0:T(8,128)S(1)} %get-tuple-element.11.centres, f32[16,8,128]{2,1,0:T(8,128)S(1)} %get-tuple-element.12.tiles, f32[16,24,256]{2,1,0:T(8,128)S(1)} %get-tuple-element.13.more, ...), custom_call_target="tpu_custom_call" | custom-call | tf_op jit(solution)/shard_map/exchange/pallas_call | solution.py:445
  53.1 1.5 %metrics.1 = (f32[1,3,2,64,256]{4,3,2,1,0:T(8,128)}, f32[1,10,2,64,256]{4,3,2,1,0:T(8,128)}) custom-call(f32[8,96,128]{2,1,0:T(8,128)S(1)} %get-tuple-element.16.own, f32[2,8,48,128]{3,2,1,0:T(8,128)S(1)} %get-tuple-element.17.halo, f32[3,2,64,256]{3,2,1,0:T(8,128)S(1)} %get-tuple-element.15.n_ref), custom_call_target="tpu_custom_call" | custom-call | tf_op jit(solution)/shard_map/metrics/pallas_call | solution.py:539
Async XLA Ops:
  1.4 31.0 %copy-start = (f32[3,2,64,256]{3,2,1,0:T(8,128)S(1)}, f32[3,2,64,256]{3,2,1,0:T(8,128)}, u32[]{:S(2)}) copy-start(f32[3,2,64,256]{3,2,1,0:T(8,128)} %n_ref.1) | copy-start | bytes 1179652
where the time goes:
time: 54.8 us; the launch traced here: 54.5 us
  Pallas kernels  53.1 us (97%)
  other arithmetic  0.75 us (1%)
  between operations  0.66 us (1%)
    pallas_call x1, Pallas kernels, gather(): pl.pallas_call(gather_kernel, out_shape=jax.ShapeDtypeStruct((BLOCKS, VAL...  31 us
    pallas_call x1, Pallas kernels, exchange(): pl.pallas_call(exchange_kernel, out_shape=(jax.ShapeDtypeStruct((INST, 96...  15.6 us
    pallas_call x1, Pallas kernels, evaluate(): pl.pallas_call(evaluate_kernel, out_shape=(shape((4 * (NC // CHUNK + 1),...  5.11 us
    pallas_call x1, Pallas kernels, metric_rows(): pl.pallas_call(metrics_kernel, out_shape=(jax.ShapeDtypeStruct((1,) + bas...  1.46 us

commit v1 on v0

--- a/solution.py
+++ b/solution.py
@@ -16,6 +16,7 @@
 BINS = 32
 CHUNK = 128
 GROUP = 8
+REACH = 4
 PLACED = 256
 GROUPS = (NC + PLACED) // 32
 MARGIN = 1.0 + 2.0**-11
@@ -47,19 +48,22 @@
     inst, space = lax.axis_index("inst"), lax.axis_index("space")
     y, core = inst // CORES, inst % CORES
     x, z = space // ZS, space % ZS
-    z_peers = [(inst, x * ZS + lax.rem(z + k, ZS)) for k in range(1, ZS)]
+
+    def along_z(d):
+        return inst, x * ZS + lax.rem(z + (d + ZS), ZS)
+
+    z_steps = [side * d for d in range(REACH, 0, -1) for side in (1, -1)]
     steps = [(a, b) for a in range(YS) for b in range(XS) if a or b]
     plane_peers = [
         (lax.rem(y + a, YS) * CORES + core, lax.rem(x + b, XS) * ZS + z) for a, b in steps
     ]
     other = (y * CORES + (1 - core), space)
 
-    def hops(a, b, c):
-        return min(a, ZS - a) + min(b, YS - b) + min(c, XS - c)
-
-    z_order = sorted(range(ZS - 1), key=lambda k: -hops(k + 1, 0, 0))
-    plane_order = sorted(range(len(steps)), key=lambda k: -hops(0, *steps[k]))
-    peers = [z_peers[k] for k in z_order] + [plane_peers[k] for k in plane_order] + [other]
+    def hops(a, b):
+        return min(a, YS - a) + min(b, XS - b)
+
+    plane_order = sorted(range(len(steps)), key=lambda k: -hops(*steps[k]))
+    peers = [along_z(d) for d in z_steps] + [plane_peers[k] for k in plane_order] + [other]
     barrier = pltpu.get_barrier_semaphore()
     for peer in peers:
         pl.semaphore_signal(barrier, inc=1, device_id=peer, device_id_type=MESH)
@@ -103,8 +107,16 @@
         copy.start()
         return copy
 
-    copies = [start(zbuf.at[z], k, z_peers[k]) for k in z_order]
-    for copy in reversed(copies):
+    copies = [start(zbuf.at[z], k, along_z(d)) for k, d in enumerate(z_steps)]
+    passed = []
+    for d, copy in reversed(list(zip(z_steps, copies))):
+        copy.wait_recv()
+        if d < REACH:
+            block = zbuf.at[lax.rem(z + (ZS - d), ZS)]
+            passed.append(start(block, len(copies) + len(passed), along_z(REACH if d > 0 else -REACH)))
+    for copy in copies:
+        copy.wait_send()
+    for copy in passed:
         copy.wait()
     rows = jnp.concatenate([zbuf[i] for i in range(ZS)], axis=0)
     rows = jnp.concatenate([rows, jnp.zeros((128 - 2 * ZS, 128), jnp.float32)], axis=0).T

time: 54.8 us -> 54.4 us (level)
    pallas_call x1, Pallas kernels: 5.11 us -> 2.54 us  [evaluate(): pl.pallas_call(evaluate_kernel, out_shape=(shape((4 * (NC // CHUNK + 1),...]
    pallas_call x1, Pallas kernels: 15.6 us -> 17.1 us  [exchange(): pl.pallas_call(exchange_kernel, out_shape=(jax.ShapeDtypeStruct((INST, 96...]
    pallas_call x1, Pallas kernels: 31 us -> 31.6 us  [gather(): pl.pallas_call(gather_kernel, out_shape=jax.ShapeDtypeStruct((BLOCKS, VAL...]
where the time goes in v1:
time: 54.4 us; the launch traced here: 54.1 us
  Pallas kernels  52.7 us (97%)
  other arithmetic  0.75 us (1%)
  between operations  0.66 us (1%)
    pallas_call x1, Pallas kernels, gather(): pl.pallas_call(gather_kernel, out_shape=jax.ShapeDtypeStruct((BLOCKS, VAL...  31.6 us
    pallas_call x1, Pallas kernels, exchange(): pl.pallas_call(exchange_kernel, out_shape=(jax.ShapeDtypeStruct((INST, 96...  17.1 us
    pallas_call x1, Pallas kernels, evaluate(): pl.pallas_call(evaluate_kernel, out_shape=(shape((4 * (NC // CHUNK + 1),...  2.54 us
    pallas_call x1, Pallas kernels, metric_rows(): pl.pallas_call(metrics_kernel, out_shape=(jax.ShapeDtypeStruct((1,) + bas...  1.46 us

profile of v1, /device:TPU:1, one launch (start us, length us, event | category | flops | bytes accessed | tf_op | source)
XLA Modules:
  0.0 54.1 jit_solution(997306928798592913)
XLA Ops:
  0.6 0.7 %select_maximum_fusion.own_ref = f32[40,40]{1,0:T(8,128)S(1)} fusion(f32[3,8]{1,0:T(4,128)} %param.6, f32[8,40]{1,0:T(8,128)} %param.4, f32[24,40]{1,0:T(8,128)} %bitcast.3), kind=kLoop, calls=%fused_computation | loop fusion | flops 6400 | bytes 11616 | tf_op jit(solution)/shard_map/concatenate | solution.py:572
  1.4 0.0 copy-start
  1.4 31.6 %gather.1.g_ref = f32[32,32,128]{2,1,0:T(8,128)S(1)} custom-call(f32[40,40]{1,0:T(8,128)S(1)} %select_maximum_fusion.own_ref), custom_call_target="tpu_custom_call" | custom-call | flops 1000000000 | bytes 20000000 | tf_op jit(solution)/shard_map/gather/pallas_call | solution.py:144
  33.0 0.0 copy-done
  33.0 2.5 %evaluate.1 = (bf16[132,48,128]{2,1,0:T(8,128)(2,1)S(1)}, f32[408,32,128]{2,1,0:T(8,128)S(1)}, f32[16,8,128]{2,1,0:T(8,128)S(1)}, f32[16,24,256]{2,1,0:T(8,128)S...) custom-call(f32[32,32,128]{2,1,0:T(8,128)S(1)} %gather.1.g_ref, f32[3,2,64,256]{3,2,1,0:T(8,128)S(1)} %copy-done), custom_call_target="tpu_custom_call" | custom-call | tf_op jit(solution)/shard_map/evaluate/pallas_call | solution.py:343
  35.5 17.1 %exchange.1 = (f32[8,96,128]{2,1,0:T(8,128)S(1)}, f32[2,8,48,128]{3,2,1,0:T(8,128)S(1)}) custom-call(bf16[132,48,128]{2,1,0:T(8,128)(2,1)S(1)} %get-tuple-element.10.windows, f32[408,32,128]{2,1,0:T(8,128)S(1)} %get-tuple-element.11.centres, f32[16,8,128]{2,1,0:T(8,128)S(1)} %get-tuple-element.12.tiles, f32[16,24,256]{2,1,0:T(8,128)S(1)} %get-tuple-element.13.more, ...), custom_call_target="tpu_custom_call" | custom-call | tf_op jit(solution)/shard_map/exchange/pallas_call | solution.py:457
  52.7 1.5 %metrics.1 = (f32[1,3,2,64,256]{4,3,2,1,0:T(8,128)}, f32[1,10,2,64,256]{4,3,2,1,0:T(8,128)}) custom-call(f32[8,96,128]{2,1,0:T(8,128)S(1)} %get-tuple-element.16.own, f32[2,8,48,128]{3,2,1,0:T(8,128)S(1)} %get-tuple-element.17.halo, f32[3,2,64,256]{3,2,1,0:T(8,128)S(1)} %get-tuple-element.15.n_ref), custom_call_target="tpu_custom_call" | custom-call | tf_op jit(solution)/shard_map/metrics/pallas_call | solution.py:551
Async XLA Ops:
  1.4 31.6 %copy-start = (f32[3,2,64,256]{3,2,1,0:T(8,128)S(1)}, f32[3,2,64,256]{3,2,1,0:T(8,128)}, u32[]{:S(2)}) copy-start(f32[3,2,64,256]{3,2,1,0:T(8,128)} %n_ref.1) | copy-start | bytes 1179652
